TPU v7x, 128 devices: a whole 4x4x4 slice. The times are simulated.
128 devices in a mesh: dp: 8 (over y_hi, x), tensor: 16 (over y_lo, z, core).
Axes of the slice: x: 4, y: 4 (y_hi: 2, y_lo: 2; y = y_hi * 2 + y_lo), z: 4, core: 2. Of those that a mesh axis runs over, the one named last changes fastest.
Arguments:
- tokens: bfloat16 [32768, 6144], P(('dp', 'tensor')), may hold values from -6 to 6
- expert_ids: int32 [32768, 2], P(('dp', 'tensor')), may hold values from 0 to 7, as said below
- slot_ids: int32 [32768, 2], P(('dp', 'tensor')), may hold values from 0 to 64, as said below
- gate_probs: float32 [32768, 2], P(('dp', 'tensor')), may hold values from 0.05 to 0.95
- gate_weight: bfloat16 [6144, 8192], P('dp', 'tensor'), may hold values from -0.078125 to 0.078125
- up_weight: bfloat16 [6144, 8192], P('dp', 'tensor'), may hold values from -0.078125 to 0.078125
- down_weight: bfloat16 [8192, 6144], P('tensor', 'dp'), may hold values from -0.0625 to 0.0625
Outputs:
- mixed: bfloat16 [32768, 6144], P(('dp', 'tensor'))
Inputs may be any that keep to these rules, and one draw needn't show every extreme that they name: `expert_ids`: each row names 2 different experts. slot_ids[t, k] counts the tokens before t in t's run of 256 that name expert expert_ids[t, k]; a count of 64 or more is given as 64, and then the token is left out of that expert's group. In some window every run has more than 64 tokens naming expert 0.
All inputs are finite; a program needn't handle non-finite values.
Results may differ from a plain program's by a relative error of at most 0.024.
Values may be sent and summed in bfloat16 or wider, within the bound.
A program may use at most 128 MiB of HBM per device.

v0:
```python
import jax
import jax.numpy as jnp
from jax import lax
from jax.sharding import PartitionSpec as P

C_DEV = 64


def body(tokens, expert_ids, slot_ids, gate_probs, gate_weight, up_weight, down_weight):
    capacity = C_DEV
    expert_hits = expert_ids == 0
    slot_grid = lax.broadcasted_iota(jnp.int32, (1, 1, capacity), 2)
    matched = expert_hits[:, :, None] & (slot_ids[:, :, None] == slot_grid)
    picker = jnp.any(matched, axis=1).astype(jnp.bfloat16)
    packed = lax.dot_general(
        picker, tokens, (((0,), (0,)), ((), ())), preferred_element_type=jnp.float32
    ).astype(jnp.bfloat16)
    combiner = jnp.sum(jnp.where(matched, gate_probs[:, :, None], 0.0), axis=1)
    group_rows = lax.all_gather(packed, "tensor", axis=0, tiled=True)
    gate_next = jnp.dot(
        group_rows,
        lax.all_gather(gate_weight, "dp", axis=0, tiled=True),
        preferred_element_type=jnp.float32,
    )
    up_next = jnp.dot(
        group_rows,
        lax.all_gather(up_weight, "dp", axis=0, tiled=True),
        preferred_element_type=jnp.float32,
    )
    hidden = (jax.nn.silu(gate_next) * up_next).astype(jnp.bfloat16)
    term_rows = jnp.dot(
        hidden,
        lax.all_gather(down_weight, "dp", axis=1, tiled=True),
        preferred_element_type=jnp.float32,
    )
    expert_rows = lax.psum_scatter(
        term_rows.astype(jnp.bfloat16), "tensor", scatter_dimension=0, tiled=True
    ).astype(jnp.float32)
    result_rows = jnp.dot(
        combiner, expert_rows, precision=lax.Precision.HIGHEST, preferred_element_type=jnp.float32
    )
    return result_rows.astype(jnp.bfloat16)


def solution(mesh):
    return jax.shard_map(
        body,
        mesh=mesh,
        in_specs=(
            P(("dp", "tensor"), None),
            P(("dp", "tensor"), None),
            P(("dp", "tensor"), None),
            P(("dp", "tensor"), None),
            P("dp", "tensor"),
            P("dp", "tensor"),
            P("tensor", "dp"),
        ),
        out_specs=P(("dp", "tensor"), None),
        check_vma=False,
    )
```

profile of v0, /device:TPU:0, one launch (start us, length us, event | category | flops | bytes accessed | tf_op | source)
XLA Modules:
  0.0 470.6 jit_solution(3475802757642831716)
XLA Ops:
  6.5 0.0 copy-start
  6.5 0.0 all-gather.7.cloned.1.call-start
  6.5 0.7 all-gather.7.cloned.1.call-update
  7.3 0.0 all-gather.5.cloned.1.call-start
  7.3 0.9 broadcast_compare_fusion
  8.2 0.7 fusion.2
  8.9 0.0 copy-done
  8.9 1.5 convolution_convert_fusion.2
  10.4 0.0 all-gather.5.cloned.1.call-update
  10.5 0.0 all-gather.11.cloned.1.call-start
  10.5 0.7 all-gather.11.cloned.1.call-update
  11.2 0.0 all-gather.9.cloned.1.call-start
  11.2 0.5 all-gather.9.cloned.1.call-update
  11.8 0.0 reduce-scatter.2.cloned.1.call-start
  11.8 90.0 %all-gather.7.cloned.1.call-done = bf16[6144,512]{1,0:T(8,128)(2,1)} async-done(((bf16[768,512]{1,0:T(8,128)(2,1)}), bf16[6144,512]{1,0:T(8,128)(2,1)}) %all-gather.7.cloned.1.call-update) | async-done | bytes 6291472 | tf_op jit(solution)/shard_map/all_gather | solution.py:22
  101.8 71.6 %all-gather.5.cloned.1.call-done = bf16[1024,6144]{1,0:T(8,128)(2,1)} async-done(((bf16[64,6144]{1,0:T(8,128)(2,1)}), bf16[1024,6144]{1,0:T(8,128)(2,1)}) %all-gather.5.cloned.1.call-update) | async-done | bytes 12582928 | tf_op jit(solution)/shard_map/all_gather | solution.py:19
  173.3 12.4 %fusion.4 = f32[1024,512]{1,0:T(8,128)} fusion(bf16[1024,6144]{1,0:T(8,128)(2,1)} %all-gather.5.cloned.1.call-done, bf16[6144,512]{1,0:T(8,128)(2,1)} %all-gather.7.cloned.1.call-done), kind=kOutput, calls=%fused_computation.11 | convolution fusion | flops 6442450944 | bytes 20971520 | tf_op jit(solution)/shard_map/dot_general | solution.py:20
  185.7 79.8 %all-gather.11.cloned.1.call-done = bf16[512,6144]{1,0:T(8,128)(2,1)} async-done(((bf16[512,768]{1,0:T(8,128)(2,1)}), bf16[512,6144]{1,0:T(8,128)(2,1)}) %all-gather.11.cloned.1.call-update) | async-done | bytes 6291472 | tf_op jit(solution)/shard_map/all_gather | solution.py:33
  265.5 89.7 %all-gather.9.cloned.1.call-done = bf16[6144,512]{1,0:T(8,128)(2,1)} async-done(((bf16[768,512]{1,0:T(8,128)(2,1)}), bf16[6144,512]{1,0:T(8,128)(2,1)}) %all-gather.9.cloned.1.call-update) | async-done | bytes 6291472 | tf_op jit(solution)/shard_map/all_gather | solution.py:27
  355.2 22.9 %convolution_convert_fusion = bf16[1024,6144]{1,0:T(8,128)(2,1)} fusion(bf16[512,6144]{1,0:T(8,128)(2,1)} %all-gather.11.cloned.1.call-done, f32[1024,512]{1,0:T(8,128)} %fusion.4, bf16[1024,6144]{1,0:T(8,128)(2,1)} %all-gather.5.cloned.1.call-done, bf16[6144,512]{1,0:T(8,128)(2,1)} %all-gather.9.cloned.1.call-done), kind=kOutput, calls=%fused_computation | convolution fusion | flops 12894339072 | bytes 39845888 | tf_op jit(solution)/shard_map/dot_general | solution.py:31
  378.1 0.0 copy-start.1
  378.1 0.0 copy-start.2
  378.1 0.0 reduce-scatter.2.cloned.1.call-update
  378.1 0.7 copy-done.1
  378.8 0.0 copy-done.2
  378.8 80.1 %reduce-scatter.2.cloned.1.call-done = bf16[64,6144]{1,0:T(8,128)(2,1)} async-done(((bf16[1024,6144]{1,0:T(8,128)(2,1)}), bf16[64,6144]{1,0:T(8,128)(2,1)}) %reduce-scatter.2.cloned.1.call-update) | async-done | bytes 786448 | tf_op jit(solution)/shard_map/reduce_scatter | solution.py:36
  458.9 5.2 %convolution_convert_fusion.1 = bf16[256,6144]{1,0:T(8,128)(2,1)} fusion(f32[256,64]{0,1:T(8,128)S(1)} %select_reduce_fusion, bf16[64,6144]{1,0:T(8,128)(2,1)} %reduce-scatter.2.cloned.1.call-done), kind=kOutput, calls=%fused_computation.1 | convolution fusion | flops 1209532416 | bytes 3997696 | tf_op jit(solution)/shard_map/dot_general | solution.py:39
  (1 shorter events, 0.0 us)
Async XLA Ops:
  6.5 2.3 copy-start
  6.5 95.2 %all-gather.7.cloned.1.call-start = ((), (), s32[]{:S(2)}) async-start(), calls=%async_computation.2 | async-start | bytes 7077888 | tf_op jit(solution)/shard_map/all_gather | solution.py:22
  7.3 166.1 %all-gather.5.cloned.1.call-start = ((), (), s32[]{:S(2)}) async-start(), calls=%async_computation.1 | async-start | bytes 13369344 | tf_op jit(solution)/shard_map/all_gather | solution.py:19
  10.5 255.0 %all-gather.11.cloned.1.call-start = ((), (), s32[]{:S(2)}) async-start(), calls=%async_computation.4 | async-start | bytes 7077888 | tf_op jit(solution)/shard_map/all_gather | solution.py:33
  11.2 344.0 %all-gather.9.cloned.1.call-start = ((), (), s32[]{:S(2)}) async-start(), calls=%async_computation.3 | async-start | bytes 7077888 | tf_op jit(solution)/shard_map/all_gather | solution.py:27
  11.8 447.2 %reduce-scatter.2.cloned.1.call-start = ((), (), s32[]{:S(2)}) async-start(), calls=%async_computation.5 | async-start | bytes 13369344 | tf_op jit(solution)/shard_map/reduce_scatter | solution.py:36
  378.1 0.7 copy-start.1
  378.1 0.7 copy-start.2
Sparse Core Ops, SparseCore 0:
  9.7 92.0 all-gather.6
  103.5 69.8 all-gather.4
  175.6 89.8 all-gather.10
  267.7 87.5 all-gather.8
  378.2 80.6 reduce-scatter.1
where the time goes:
time: 471 us
  waiting for transfers between devices  413 us (88%)
  matrix products  42 us (9%)
  between operations  13.2 us (3%)
    all_gather x1, waiting for transfers between devices, body(): lax.all_gather(gate_weight, 'dp', axis=0, tiled=True)  90 us
    all_gather x1, waiting for transfers between devices, body(): lax.all_gather(up_weight, 'dp', axis=0, tiled=True)  89.7 us
    reduce_scatter x1, waiting for transfers between devices, body(): lax.psum_scatter(term_rows.astype(jnp.bfloat16), 'tensor', scatter_dimens...  80.1 us
    all_gather x1, waiting for transfers between devices, body(): lax.all_gather(down_weight, 'dp', axis=1, tiled=True)  79.8 us
    all_gather x1, waiting for transfers between devices, body(): group_rows = lax.all_gather(packed, 'tensor', axis=0, tiled=True)  71.6 us
    dot_general x1, matrix products, body(): jnp.dot(hidden, lax.all_gather(down_weight, 'dp', axis=1, tiled=True), pr...  22.9 us
    dot_general x1, matrix products, body(): jnp.dot(group_rows, lax.all_gather(gate_weight, 'dp', axis=0, tiled=True)...  12.4 us
  transfers between devices with their start and end apart: 5, of which 5 were waited for; matrix products, arithmetic and copies ran while one was open for 3% of the time, Pallas kernels for 0%

commit v1 on v0

v1 whole, which is shorter than its diff:
```python
import functools

import jax
import jax.numpy as jnp
from jax import lax
from jax.experimental import pallas as pl
from jax.experimental.pallas import tpu as pltpu
from jax.sharding import PartitionSpec as P

MESH = pl.DeviceIdType.MESH
F32 = jnp.float32
BF16 = jnp.bfloat16

SLOTS = 64
RUN = 256
DEPTH = 768
UNITS = 512
ROWS = 1024
SHARDS = 8
SPLIT = 512
COPIES = 112

ORDER = (0, 4, 1, 3, 5, 7, 2, 6)


def place():
    dp, tensor = lax.axis_index("dp"), lax.axis_index("tensor")
    return dp // 4, dp % 4, tensor // 8, (tensor // 2) % 4, tensor % 2


def device(d_yh, d_x, d_yl, d_z, d_c):
    yh, x, yl, z, c = place()
    yh, x, yl, z, c = (yh + d_yh) % 2, (x + d_x) % 4, (yl + d_yl) % 2, (z + d_z) % 4, (c + d_c) % 2
    return (yh * 4 + x, yl * 8 + z * 2 + c)


def shard_columns(s):
    yh, x, _, _, _ = place()
    owner = ((yh + s // 4) % 2) * 4 + (x + s % 4) % 4
    return pl.ds(pl.multiple_of(owner * DEPTH, DEPTH), DEPTH)


def kernel(
    tok_hbm, ids_ref, slots_ref, probs_ref, wg_hbm, wu_hbm, wd_hbm, out_hbm,
    xbuf, wg, wu, wd, accg, accu, hid, c1r, z2r, z1r, q, f0, yr, ost, send_sem, recv_sem, local_sem,
):
    XP, XM = device(0, 1, 0, 0, 0), device(0, 3, 0, 0, 0)
    Y2, YN = device(1, 0, 0, 0, 0), device(0, 0, 1, 0, 0)
    ZP, ZM = device(0, 0, 0, 1, 0), device(0, 0, 0, 3, 0)
    CORE = device(0, 0, 0, 0, 1)
    started = []

    def send(src, dst, to):
        i = len(started)
        copy = pltpu.make_async_remote_copy(
            src_ref=src, dst_ref=dst, send_sem=send_sem.at[i], recv_sem=recv_sem.at[i],
            device_id=to, device_id_type=MESH,
        )
        copy.start()
        started.append(copy)
        return copy

    tok_loads = []
    for s in range(SHARDS):
        load = pltpu.make_async_copy(tok_hbm.at[:, shard_columns(s)], c1r.at[s, pl.ds(0, RUN)], local_sem.at[s])
        load.start()
        tok_loads.append(load)
    own_loads = []
    for k, (src, dst) in enumerate(((wg_hbm, wg), (wu_hbm, wu), (wd_hbm, wd))):
        load = pltpu.make_async_copy(src, dst.at[0], local_sem.at[8 + k])
        load.start()
        own_loads.append(load)

    barrier = pltpu.get_barrier_semaphore()
    for to in (XP, XM, Y2, YN, ZP, ZM, CORE):
        pl.semaphore_signal(barrier, inc=1, device_id=to, device_id_type=MESH)
    pl.semaphore_wait(barrier, 7)

    g_x = (send(wg_hbm, wg.at[3], XP), send(wg_hbm, wg.at[1], XM))
    u_x = (send(wu_hbm, wu.at[3], XP), send(wu_hbm, wu.at[1], XM))

    hit0, hit1 = ids_ref[:, 0:1] == 0, ids_ref[:, 1:2] == 0
    slot = jnp.minimum(
        jnp.where(hit0, slots_ref[:, 0:1], SLOTS), jnp.where(hit1, slots_ref[:, 1:2], SLOTS)
    )
    weight = jnp.where(hit0, probs_ref[:, 0:1], 0.0) + jnp.where(hit1, probs_ref[:, 1:2], 0.0)
    lane = lax.broadcasted_iota(jnp.int32, (RUN, 2 * SLOTS), 1)
    lane = jnp.where(lane >= SLOTS, lane - SLOTS, lane)
    picker = jnp.where(lane == slot, 1.0, 0.0)
    picker_t = picker.T[:SLOTS].astype(BF16)
    for s in range(SHARDS):
        tok_loads[s].wait()
        xbuf[s, pl.ds(0, SLOTS), :] = jnp.dot(
            picker_t, c1r[s, pl.ds(0, RUN), :], preferred_element_type=F32
        ).astype(BF16)

    def block(rc, ryl, rz, half=None):
        at = pl.ds(rc * 512 + ryl * 256 + rz * 64, 64)
        if half is None:
            return xbuf.at[:, at]
        return xbuf.at[pl.ds(half * 4, 4), at]

    to_core = []

    def core(ryl, rz, half=None):
        to_core.append(send(block(0, ryl, rz, half), block(1, ryl, rz, half), CORE))

    x_y = send(block(0, 0, 0), block(0, 1, 0), YN)
    x_z = (send(block(0, 0, 0), block(0, 0, 3), ZP), send(block(0, 0, 0), block(0, 0, 1), ZM))
    core(0, 0)
    g_y = send(wg_hbm, wg.at[4], Y2)
    u_y = send(wu_hbm, wu.at[4], Y2)

    lo, hi = pl.ds(0, 384), pl.ds(384, 384)
    ring, rest = pl.ds(0, SPLIT), pl.ds(SPLIT, DEPTH - SPLIT)
    ring_lo, ring_hi = pl.ds(0, SPLIT // 2), pl.ds(SPLIT // 2, SPLIT // 2)

    def relay_own(w, first):
        first[0].wait_recv()
        a = send(w.at[3, lo], w.at[2, lo], XP)
        first[1].wait_recv()
        b = send(w.at[1, hi], w.at[2, hi], XM)
        c = send(w.at[3, rest], w.at[7, rest], Y2)
        d = send(w.at[1, rest], w.at[5, rest], Y2)
        return a, b, c, d

    def ring_partner(w, first):
        first.wait_recv()
        return send(w.at[4, ring], w.at[7, ring], XP), send(w.at[4, ring], w.at[5, ring], XM)

    def relay_partner(w, first):
        first[0].wait_recv()
        a = send(w.at[7, ring_lo], w.at[6, ring_lo], XP)
        first[1].wait_recv()
        return a, send(w.at[5, ring_hi], w.at[6, ring_hi], XM)

    g_r = relay_own(wg, g_x)
    x_z[0].wait_recv()
    x_zr = [send(block(0, 0, 3, 0), block(0, 0, 2, 0), ZP)]
    core(0, 3)
    x_z[1].wait_recv()
    x_zr.append(send(block(0, 0, 1, 1), block(0, 0, 2, 1), ZM))
    core(0, 1)
    x_y.wait_recv()
    x_yz = (send(block(0, 1, 0), block(0, 1, 3), ZP), send(block(0, 1, 0), block(0, 1, 1), ZM))
    core(1, 0)
    g_p = ring_partner(wg, g_y)
    for half in (0, 1):
        x_zr[half].wait_recv()
        core(0, 2, half)
    u_r = relay_own(wu, u_x)
    x_yz[0].wait_recv()
    x_yzr = [send(block(0, 1, 3, 0), block(0, 1, 2, 0), ZP)]
    core(1, 3)
    x_yz[1].wait_recv()
    x_yzr.append(send(block(0, 1, 1, 1), block(0, 1, 2, 1), ZM))
    core(1, 1)

    def far_rest(w, relays):
        relays[0].wait_recv()
        relays[1].wait_recv()
        return send(w.at[2, rest], w.at[6, rest], Y2)

    g_f = far_rest(wg, g_r)
    u_p = ring_partner(wu, u_y)
    for half in (0, 1):
        x_yzr[half].wait_recv()
        core(1, 2, half)
    u_f = far_rest(wu, u_r)
    d_y = send(wd_hbm, wd.at[4], Y2)
    for copy in to_core:
        copy.wait_recv()

    def gemm(acc, w, s, first=False):
        @pl.loop(0, 2)
        def _(m):
            rows = pl.ds(pl.multiple_of(m * 512, 512), 512)
            part = jnp.dot(xbuf[s, rows, :], w[s], preferred_element_type=F32)
            if first:
                acc[rows, :] = part
            else:
                acc[rows, :] += part

    own_loads[0].wait()
    own_loads[1].wait()
    gemm(accg, wg, 0, True)
    gemm(accu, wu, 0, True)
    gemm(accg, wg, 1)
    gemm(accg, wg, 3)
    gemm(accg, wg, 4)
    gemm(accg, wg, 2)
    g_pr = relay_partner(wg, g_p)
    gemm(accu, wu, 1)
    gemm(accu, wu, 3)
    gemm(accu, wu, 4)
    gemm(accu, wu, 2)
    u_pr = relay_partner(wu, u_p)
    d_x = (send(wd_hbm, wd.at[3], XP), send(wd_hbm, wd.at[1], XM))
    d_y.wait_recv()
    d_p = (send(wd.at[4], wd.at[7], XP), send(wd.at[4], wd.at[5], XM))
    g_r[2].wait_recv()
    gemm(accg, wg, 7)
    g_r[3].wait_recv()
    gemm(accg, wg, 5)
    u_r[2].wait_recv()
    gemm(accu, wu, 7)
    u_r[3].wait_recv()
    gemm(accu, wu, 5)
    for copy in (g_f, *g_pr):
        copy.wait_recv()
    gemm(accg, wg, 6)
    for copy in (u_f, *u_pr):
        copy.wait_recv()
    gemm(accu, wu, 6)

    @pl.loop(0, 4)
    def _(m):
        rows = pl.ds(pl.multiple_of(m * 256, 256), 256)
        gate = accg[rows, :]
        hid[rows, :] = (gate / (1.0 + jnp.exp(-gate)) * accu[rows, :]).astype(BF16)

    for copy in (x_y, *x_z, *x_zr, *x_yz, *x_yzr, *to_core):
        copy.wait_send()

    d_lo, d_hi = pl.ds(0, 256), pl.ds(256, 256)
    c1, z2, z1, y1, outs = {}, {}, {}, {}, {}
    d_r, d_pr = [], []

    def down_ready(s):
        if s == 0:
            own_loads[2].wait()
        elif s == 1:
            d_x[0].wait_recv()
            d_x[1].wait_recv()
            d_r.append(send(wd.at[3, d_lo], wd.at[2, d_lo], XP))
            d_r.append(send(wd.at[1, d_hi], wd.at[2, d_hi], XM))
        elif s == 5:
            d_p[0].wait_recv()
            d_p[1].wait_recv()
            d_pr.append(send(wd.at[7, d_lo], wd.at[6, d_lo], XP))
            d_pr.append(send(wd.at[5, d_hi], wd.at[6, d_hi], XM))
        elif s == 2:
            for copy in d_r:
                copy.wait_recv()
        elif s == 6:
            for copy in d_pr:
                copy.wait_recv()

    def step_core(s):
        down_ready(s)

        @pl.loop(0, 2)
        def _(m):
            rows = pl.ds(pl.multiple_of(512 + m * 256, 256), 256)
            xbuf[s, rows, :] = jnp.dot(hid[rows, :], wd[s], preferred_element_type=F32).astype(BF16)

        c1[s] = send(xbuf.at[s, pl.ds(512, 512)], c1r.at[s], CORE)

    def step_far(i, s):
        c1[s].wait_recv()

        @pl.loop(0, 2)
        def _(m):
            rows = pl.ds(pl.multiple_of(m * 256, 256), 256)
            at = pl.ds(pl.multiple_of(m * 64, 64), 64)
            part = jnp.dot(hid[rows, :], wd[s], preferred_element_type=F32) + c1r[s, rows, :].astype(F32)
            q[i % 3, 0, at, :] = part[0:64]
            q[i % 3, 1, at, :] = part[64:128]
            q[i % 3, 2, at, :] = part[192:256]
            xbuf[s, pl.ds(pl.multiple_of(256 + m * 64, 64), 64), :] = part[128:192].astype(BF16)

        z2[s] = (
            send(xbuf.at[s, pl.ds(256, 128), lo], z2r.at[s, 0], ZP),
            send(xbuf.at[s, pl.ds(256, 128), hi], z2r.at[s, 1], ZM),
        )

    def step_near(i, s):
        z2[s][0].wait_recv()
        z2[s][1].wait_recv()
        xbuf[s, 0:128, 0:384] = (q[i % 3, 1, :, 0:384] + z2r[s, 0].astype(F32)).astype(BF16)
        xbuf[s, 0:128, 384:768] = q[i % 3, 1, :, 384:768].astype(BF16)
        xbuf[s, 128:256, 0:384] = q[i % 3, 2, :, 0:384].astype(BF16)
        xbuf[s, 128:256, 384:768] = (q[i % 3, 2, :, 384:768] + z2r[s, 1].astype(F32)).astype(BF16)
        z1[s] = (
            send(xbuf.at[s, pl.ds(0, 128)], z1r.at[s, 0], ZP),
            send(xbuf.at[s, pl.ds(128, 128)], z1r.at[s, 1], ZM),
        )

    def step_y(i, s):
        z1[s][0].wait_recv()
        z1[s][1].wait_recv()
        total = q[i % 3, 0] + z1r[s, 0].astype(F32) + z1r[s, 1].astype(F32)
        f0[i % 2] = total[0:64]
        xbuf[s, 384:448, :] = total[64:128].astype(BF16)
        y1[s] = send(xbuf.at[s, pl.ds(384, 64)], yr.at[s], YN)

    def step_out(i, s):
        y1[s].wait_recv()
        rows = f0[i % 2] + yr[s].astype(F32)
        head = rows.astype(BF16)
        tail = (rows - head.astype(F32)).astype(BF16)
        mixed = weight * jnp.dot(
            picker.astype(BF16), jnp.concatenate([head, tail], axis=0), preferred_element_type=F32
        )
        if i >= 2:
            outs[i - 2].wait()
        ost[i % 2] = mixed.astype(BF16)
        outs[i] = pltpu.make_async_copy(ost.at[i % 2], out_hbm.at[:, shard_columns(s)], local_sem.at[11 + i])
        outs[i].start()

    for i in range(SHARDS + 4):
        if i < SHARDS:
            step_core(ORDER[i])
        if 0 <= i - 1 < SHARDS:
            step_far(i - 1, ORDER[i - 1])
        if 0 <= i - 2 < SHARDS:
            step_near(i - 2, ORDER[i - 2])
        if 0 <= i - 3 < SHARDS:
            step_y(i - 3, ORDER[i - 3])
        if 0 <= i - 4 < SHARDS:
            step_out(i - 4, ORDER[i - 4])

    outs[SHARDS - 2].wait()
    outs[SHARDS - 1].wait()
    waited = (x_y, *x_z, *x_zr, *x_yz, *x_yzr, *to_core)
    for copy in started:
        if not any(copy is other for other in waited):
            copy.wait_send()


def body(tokens, expert_ids, slot_ids, gate_probs, gate_weight, up_weight, down_weight):
    hbm, vmem = pl.BlockSpec(memory_space=pl.ANY), pl.BlockSpec(memory_space=pltpu.VMEM)
    return pl.pallas_call(
        kernel,
        out_shape=jax.ShapeDtypeStruct(tokens.shape, BF16),
        in_specs=[hbm, vmem, vmem, vmem, hbm, hbm, hbm],
        out_specs=hbm,
        scratch_shapes=[
            pltpu.VMEM((SHARDS, ROWS, DEPTH), BF16),
            pltpu.VMEM((SHARDS, DEPTH, UNITS), BF16),
            pltpu.VMEM((SHARDS, DEPTH, UNITS), BF16),
            pltpu.VMEM((SHARDS, UNITS, DEPTH), BF16),
            pltpu.VMEM((ROWS, UNITS), F32),
            pltpu.VMEM((ROWS, UNITS), F32),
            pltpu.VMEM((ROWS, UNITS), BF16),
            pltpu.VMEM((SHARDS, 512, DEPTH), BF16),
            pltpu.VMEM((SHARDS, 2, 128, 384), BF16),
            pltpu.VMEM((SHARDS, 2, 128, DEPTH), BF16),
            pltpu.VMEM((3, 3, 128, DEPTH), F32),
            pltpu.VMEM((2, SLOTS, DEPTH), F32),
            pltpu.VMEM((SHARDS, SLOTS, DEPTH), BF16),
            pltpu.VMEM((2, RUN, DEPTH), BF16),
            pltpu.SemaphoreType.DMA((COPIES,)),
            pltpu.SemaphoreType.DMA((COPIES,)),
            pltpu.SemaphoreType.DMA((20,)),
        ],
        compiler_params=pltpu.CompilerParams(
            collective_id=0, has_side_effects=True, vmem_limit_bytes=62 << 20
        ),
        cost_estimate=pl.CostEstimate(flops=20_000_000_000, bytes_accessed=60_000_000, transcendentals=1_000_000),
    )(tokens, expert_ids, slot_ids, gate_probs, gate_weight, up_weight, down_weight)


def solution(mesh):
    return jax.shard_map(
        body,
        mesh=mesh,
        in_specs=(
            P(("dp", "tensor"), None),
            P(("dp", "tensor"), None),
            P(("dp", "tensor"), None),
            P(("dp", "tensor"), None),
            P("dp", "tensor"),
            P("dp", "tensor"),
            P("tensor", "dp"),
        ),
        out_specs=P(("dp", "tensor"), None),
        check_vma=False,
    )
```

time: 471 us -> 193 us (0.41)
  waiting for transfers between devices: 413 us -> 0 us
  Pallas kernels: 0 us -> 183 us
  matrix products: 42 us -> 0 us
  between operations: 13.2 us -> 0.01 us
  local copies, waits for them, and re-layouts: 0.68 us -> 8.29 us
    all_gather x4 -> x0, waiting for transfers between devices: 331 us -> none  [the longest x1 90 us: body(): lax.all_gather(gate_weight, 'dp', axis=0, tiled=True)]
    pallas_call x0 -> x1, Pallas kernels: none -> 183 us  [body(): pl.pallas_call(kernel, out_shape=jax.ShapeDtypeStruct(tokens.shape, BF16)...]
    reduce_scatter x1 -> x0, waiting for transfers between devices: 80.1 us -> none  [body(): lax.psum_scatter(term_rows.astype(jnp.bfloat16), 'tensor', scatter_dimens...]
    dot_general x4 -> x0, matrix products: 42 us -> none  [the longest x1 22.9 us: body(): jnp.dot(hidden, lax.all_gather(down_weight, 'dp', axis=1, tiled=True), pr...]
    unnamed x6 -> x4, local copies, waits for them, and re-layouts: 0.68 us -> 8.29 us
  transfers between devices with their start and end apart: 5 -> 0, of which waited for: 5 -> 0; matrix products, arithmetic and copies ran while one was open for 3% -> 0% of each run, Pallas kernels for 0% -> 0%
where the time goes in v1:
time: 193 us; the launch traced here: 192 us
  Pallas kernels  183 us (95%)
  local copies, waits for them, and re-layouts  8.29 us (4%)
    pallas_call x1, Pallas kernels, body(): pl.pallas_call(kernel, out_shape=jax.ShapeDtypeStruct(tokens.shape, BF16)...  183 us
    unnamed x4, local copies, waits for them, and re-layouts  8.29 us

profile of v1, /device:TPU:0, one launch (start us, length us, event | category | flops | bytes accessed | tf_op | source)
XLA Modules:
  0.0 191.6 jit_solution(1694481418409416529)
XLA Ops:
  0.0 1.5 copy.8.ids_ref
  1.5 1.5 copy.9.slots_ref
  2.9 1.5 copy.10.probs_ref
  4.4 183.3 %shard_map.73 = bf16[256,6144]{1,0:T(8,128)(2,1)} custom-call(bf16[256,6144]{1,0:T(8,128)(2,1)} %tok_hbm.1, s32[256,2]{1,0:T(8,128)} %copy.8.ids_ref, s32[256,2]{1,0:T(8,128)} %copy.9.slots_ref, f32[256,2]{1,0:T(8,128)} %copy.10.probs_ref, bf16[768,512]{1,0:T(8,128)(2,1)} %wg_hbm.1, bf16[768,512]{1,0:T(8,128)(2,1)} %wu_hbm.1, bf16[512,768]{1,0:T(8,128)(2,1)} %wd_hbm.1), custom_call_target="tpu_custom_call" | custom-call | flops 20000000000 | bytes 60000000 | tf_op jit(solution)/shard_map/pallas_call | solution.py:333
  187.7 3.9 %copy.12 = bf16[256,6144]{1,0:T(8,128)(2,1)} copy(bf16[256,6144]{1,0:T(8,128)(2,1)} %shard_map.73) | data formatting | bytes 6291456

commit v2 on v1

--- a/solution.py
+++ b/solution.py
@@ -17,7 +17,7 @@
 UNITS = 512
 ROWS = 1024
 SHARDS = 8
-SPLIT = 512
+SPLIT = 528
 COPIES = 112
 
 ORDER = (0, 4, 1, 3, 5, 7, 2, 6)
@@ -40,9 +40,29 @@
     return pl.ds(pl.multiple_of(owner * DEPTH, DEPTH), DEPTH)
 
 
+def slot_row(ids_ref, slots_ref):
+    first = jnp.where(ids_ref[0:1, :] == 0, slots_ref[0:1, :], SLOTS)
+    return jnp.minimum(first, jnp.where(ids_ref[1:2, :] == 0, slots_ref[1:2, :], SLOTS))
+
+
+def combine(ids_ref, slots_ref, probs_ref, rows_ref, mixed_ref):
+    row = lax.broadcasted_iota(jnp.int32, (2 * SLOTS, RUN), 0)
+    row = jnp.where(row >= SLOTS, row - SLOTS, row)
+    picked = row == slot_row(ids_ref, slots_ref)
+    weight = jnp.where(ids_ref[0:1, :] == 0, probs_ref[0:1, :], 0.0)
+    weight += jnp.where(ids_ref[1:2, :] == 0, probs_ref[1:2, :], 0.0)
+    picker = jnp.where(picked, 1.0, 0.0).T.astype(BF16)
+    weight = jnp.sum(jnp.where(picked, weight, 0.0).T[:, :SLOTS], axis=1, keepdims=True)
+    rows = rows_ref[...]
+    head = rows.astype(BF16)
+    tail = (rows - head.astype(F32)).astype(BF16)
+    both = jnp.concatenate([head, tail], axis=0)
+    mixed_ref[...] = (weight * jnp.dot(picker, both, preferred_element_type=F32)).astype(BF16)
+
+
 def kernel(
-    tok_hbm, ids_ref, slots_ref, probs_ref, wg_hbm, wu_hbm, wd_hbm, out_hbm,
-    xbuf, wg, wu, wd, accg, accu, hid, c1r, z2r, z1r, q, f0, yr, ost, send_sem, recv_sem, local_sem,
+    tok_hbm, ids_ref, slots_ref, wg_hbm, wu_hbm, wd_hbm, out_hbm,
+    xbuf, wg, wu, wd, accg, accu, hid, c1r, z2r, z1r, q, f0, yr, send_sem, recv_sem, local_sem,
 ):
     XP, XM = device(0, 1, 0, 0, 0), device(0, 3, 0, 0, 0)
     Y2, YN = device(1, 0, 0, 0, 0), device(0, 0, 1, 0, 0)
@@ -79,15 +99,10 @@
     g_x = (send(wg_hbm, wg.at[3], XP), send(wg_hbm, wg.at[1], XM))
     u_x = (send(wu_hbm, wu.at[3], XP), send(wu_hbm, wu.at[1], XM))
 
-    hit0, hit1 = ids_ref[:, 0:1] == 0, ids_ref[:, 1:2] == 0
-    slot = jnp.minimum(
-        jnp.where(hit0, slots_ref[:, 0:1], SLOTS), jnp.where(hit1, slots_ref[:, 1:2], SLOTS)
-    )
-    weight = jnp.where(hit0, probs_ref[:, 0:1], 0.0) + jnp.where(hit1, probs_ref[:, 1:2], 0.0)
-    lane = lax.broadcasted_iota(jnp.int32, (RUN, 2 * SLOTS), 1)
-    lane = jnp.where(lane >= SLOTS, lane - SLOTS, lane)
-    picker = jnp.where(lane == slot, 1.0, 0.0)
-    picker_t = picker.T[:SLOTS].astype(BF16)
+    g_y = send(wg_hbm.at[pl.ds(0, 384)], wg.at[4, pl.ds(0, 384)], Y2)
+
+    row = lax.broadcasted_iota(jnp.int32, (SLOTS, RUN), 0)
+    picker_t = jnp.where(row == slot_row(ids_ref, slots_ref), 1.0, 0.0).astype(BF16)
     for s in range(SHARDS):
         tok_loads[s].wait()
         xbuf[s, pl.ds(0, SLOTS), :] = jnp.dot(
@@ -108,12 +123,12 @@
     x_y = send(block(0, 0, 0), block(0, 1, 0), YN)
     x_z = (send(block(0, 0, 0), block(0, 0, 3), ZP), send(block(0, 0, 0), block(0, 0, 1), ZM))
     core(0, 0)
-    g_y = send(wg_hbm, wg.at[4], Y2)
-    u_y = send(wu_hbm, wu.at[4], Y2)
+    g_y = (g_y, send(wg_hbm.at[pl.ds(384, 384)], wg.at[4, pl.ds(384, 384)], Y2))
+    u_y = (send(wu_hbm, wu.at[4], Y2),)
 
     lo, hi = pl.ds(0, 384), pl.ds(384, 384)
     ring, rest = pl.ds(0, SPLIT), pl.ds(SPLIT, DEPTH - SPLIT)
-    ring_lo, ring_hi = pl.ds(0, SPLIT // 2), pl.ds(SPLIT // 2, SPLIT // 2)
+    ring_lo, ring_hi = pl.ds(0, 272), pl.ds(272, SPLIT - 272)
 
     def relay_own(w, first):
         first[0].wait_recv()
@@ -125,7 +140,8 @@
         return a, b, c, d
 
     def ring_partner(w, first):
-        first.wait_recv()
+        for copy in first:
+            copy.wait_recv()
         return send(w.at[4, ring], w.at[7, ring], XP), send(w.at[4, ring], w.at[5, ring], XM)
 
     def relay_partner(w, first):
@@ -290,22 +306,14 @@
         z1[s][0].wait_recv()
         z1[s][1].wait_recv()
         total = q[i % 3, 0] + z1r[s, 0].astype(F32) + z1r[s, 1].astype(F32)
-        f0[i % 2] = total[0:64]
+        f0[i] = total[0:64]
         xbuf[s, 384:448, :] = total[64:128].astype(BF16)
         y1[s] = send(xbuf.at[s, pl.ds(384, 64)], yr.at[s], YN)
 
     def step_out(i, s):
         y1[s].wait_recv()
-        rows = f0[i % 2] + yr[s].astype(F32)
-        head = rows.astype(BF16)
-        tail = (rows - head.astype(F32)).astype(BF16)
-        mixed = weight * jnp.dot(
-            picker.astype(BF16), jnp.concatenate([head, tail], axis=0), preferred_element_type=F32
-        )
-        if i >= 2:
-            outs[i - 2].wait()
-        ost[i % 2] = mixed.astype(BF16)
-        outs[i] = pltpu.make_async_copy(ost.at[i % 2], out_hbm.at[:, shard_columns(s)], local_sem.at[11 + i])
+        f0[i] += yr[s].astype(F32)
+        outs[i] = pltpu.make_async_copy(f0.at[i], out_hbm.at[:, shard_columns(s)], local_sem.at[11 + i])
         outs[i].start()
 
     for i in range(SHARDS + 4):
@@ -320,8 +328,8 @@
         if 0 <= i - 4 < SHARDS:
             step_out(i - 4, ORDER[i - 4])
 
-    outs[SHARDS - 2].wait()
-    outs[SHARDS - 1].wait()
+    for copy in outs.values():
+        copy.wait()
     waited = (x_y, *x_z, *x_zr, *x_yz, *x_yzr, *to_core)
     for copy in started:
         if not any(copy is other for other in waited):
@@ -330,10 +338,11 @@
 
 def body(tokens, expert_ids, slot_ids, gate_probs, gate_weight, up_weight, down_weight):
     hbm, vmem = pl.BlockSpec(memory_space=pl.ANY), pl.BlockSpec(memory_space=pltpu.VMEM)
-    return pl.pallas_call(
+    ids, slots, probs = expert_ids.T, slot_ids.T, gate_probs.T
+    rows = pl.pallas_call(
         kernel,
-        out_shape=jax.ShapeDtypeStruct(tokens.shape, BF16),
-        in_specs=[hbm, vmem, vmem, vmem, hbm, hbm, hbm],
+        out_shape=jax.ShapeDtypeStruct((SLOTS, tokens.shape[1]), F32),
+        in_specs=[hbm, vmem, vmem, hbm, hbm, hbm],
         out_specs=hbm,
         scratch_shapes=[
             pltpu.VMEM((SHARDS, ROWS, DEPTH), BF16),
@@ -347,9 +356,8 @@
             pltpu.VMEM((SHARDS, 2, 128, 384), BF16),
             pltpu.VMEM((SHARDS, 2, 128, DEPTH), BF16),
             pltpu.VMEM((3, 3, 128, DEPTH), F32),
-            pltpu.VMEM((2, SLOTS, DEPTH), F32),
+            pltpu.VMEM((SHARDS, SLOTS, DEPTH), F32),
             pltpu.VMEM((SHARDS, SLOTS, DEPTH), BF16),
-            pltpu.VMEM((2, RUN, DEPTH), BF16),
             pltpu.SemaphoreType.DMA((COPIES,)),
             pltpu.SemaphoreType.DMA((COPIES,)),
             pltpu.SemaphoreType.DMA((20,)),
@@ -358,7 +366,15 @@
             collective_id=0, has_side_effects=True, vmem_limit_bytes=62 << 20
         ),
         cost_estimate=pl.CostEstimate(flops=20_000_000_000, bytes_accessed=60_000_000, transcendentals=1_000_000),
-    )(tokens, expert_ids, slot_ids, gate_probs, gate_weight, up_weight, down_weight)
+    )(tokens, ids, slots, gate_weight, up_weight, down_weight)
+    whole = pl.BlockSpec((2, RUN), lambda i: (0, 0))
+    return pl.pallas_call(
+        combine,
+        grid=(4,),
+        out_shape=jax.ShapeDtypeStruct(tokens.shape, BF16),
+        in_specs=[whole, whole, whole, pl.BlockSpec((SLOTS, 2 * DEPTH), lambda i: (0, i))],
+        out_specs=pl.BlockSpec((RUN, 2 * DEPTH), lambda i: (0, i)),
+    )(ids, slots, probs, rows)
 
 
 def solution(mesh):

time: 193 us -> 185 us (0.959)
  local copies, waits for them, and re-layouts: 8.29 us -> 0 us
    unnamed x4 -> x0, local copies, waits for them, and re-layouts: 8.29 us -> none
    pallas_call x1 -> x2, Pallas kernels: 183 us -> 184 us  [the longest x1 179 us: body(): pl.pallas_call(kernel, out_shape=jax.ShapeDtypeStruct((SLOTS, tokens.shap...]
where the time goes in v2:
time: 185 us; the launch traced here: 184 us
  Pallas kernels  184 us (99%)
    pallas_call x1, Pallas kernels, body(): pl.pallas_call(kernel, out_shape=jax.ShapeDtypeStruct((SLOTS, tokens.shap...  179 us
    pallas_call x1, Pallas kernels, body(): pl.pallas_call(combine, grid=(4,), out_shape=jax.ShapeDtypeStruct(tokens....  4.66 us

profile of v2, /device:TPU:0, one launch (start us, length us, event | category | flops | bytes accessed | tf_op | source)
XLA Modules:
  0.0 183.5 jit_solution(12899795320015084227)
XLA Ops:
  0.0 178.8 %shard_map.73.rows_ref = f32[64,6144]{1,0:T(8,128)} custom-call(bf16[256,6144]{1,0:T(8,128)(2,1)} %tok_hbm.1, s32[2,256]{1,0:T(2,128)} %bitcast.3, s32[2,256]{1,0:T(2,128)} %bitcast.5, bf16[768,512]{1,0:T(8,128)(2,1)} %wg_hbm.1, bf16[768,512]{1,0:T(8,128)(2,1)} %wu_hbm.1, bf16[512,768]{1,0:T(8,128)(2,1)} %wd_hbm.1), custom_call_target="tpu_custom_call" | custom-call | flops 20000000000 | bytes 60000000 | tf_op jit(solution)/shard_map/pallas_call | solution.py:342
  178.9 4.7 %shard_map.74 = bf16[256,6144]{1,0:T(8,128)(2,1)} custom-call(s32[2,256]{1,0:T(2,128)} %bitcast.4, s32[2,256]{1,0:T(2,128)} %bitcast.6, f32[2,256]{1,0:T(2,128)} %bitcast.7, f32[64,6144]{1,0:T(8,128)} %shard_map.73.rows_ref), custom_call_target="tpu_custom_call" | custom-call | tf_op jit(solution)/shard_map/pallas_call | solution.py:371

commit v3 on v0

v3 whole, which is shorter than its diff:
```python
import functools

import jax
import jax.numpy as jnp
from jax import lax
from jax.experimental import pallas as pl
from jax.experimental.pallas import tpu as pltpu
from jax.sharding import PartitionSpec as P

MESH = pl.DeviceIdType.MESH
F32 = jnp.float32
BF16 = jnp.bfloat16

SLOTS = 64
RUN = 256
DEPTH = 768
UNITS = 512
ROWS = 1024
SHARDS = 8
COPIES = 144
CORE_SENDS = 16


def place():
    dp, tensor = lax.axis_index("dp"), lax.axis_index("tensor")
    return dp // 4, dp % 4, tensor // 8, (tensor // 2) % 4, tensor % 2


def device(d_yh, d_x, d_yl, d_z, d_c):
    yh, x, yl, z, c = place()
    yh, x, yl, z, c = (yh + d_yh) % 2, (x + d_x) % 4, (yl + d_yl) % 2, (z + d_z) % 4, (c + d_c) % 2
    return (yh * 4 + x, yl * 8 + z * 2 + c)


def shard_columns(s):
    yh, x, _, _, _ = place()
    owner = ((yh + s // 4) % 2) * 4 + (x + s % 4) % 4
    return pl.ds(pl.multiple_of(owner * DEPTH, DEPTH), DEPTH)


def slot_row(ids_ref, slots_ref):
    first = jnp.where(ids_ref[0:1, :] == 0, slots_ref[0:1, :], SLOTS)
    return jnp.minimum(first, jnp.where(ids_ref[1:2, :] == 0, slots_ref[1:2, :], SLOTS))


def combine(ids_ref, slots_ref, probs_ref, rows_ref, mixed_ref):
    row = lax.broadcasted_iota(jnp.int32, (2 * SLOTS, RUN), 0)
    row = jnp.where(row >= SLOTS, row - SLOTS, row)
    picked = row == slot_row(ids_ref, slots_ref)
    weight = jnp.where(ids_ref[0:1, :] == 0, probs_ref[0:1, :], 0.0)
    weight += jnp.where(ids_ref[1:2, :] == 0, probs_ref[1:2, :], 0.0)
    picker = jnp.where(picked, 1.0, 0.0).T.astype(BF16)
    weight = jnp.sum(jnp.where(picked, weight, 0.0).T[:, :SLOTS], axis=1, keepdims=True)
    rows = rows_ref[...]
    head = rows.astype(BF16)
    tail = (rows - head.astype(F32)).astype(BF16)
    both = jnp.concatenate([head, tail], axis=0)
    mixed_ref[...] = (weight * jnp.dot(picker, both, preferred_element_type=F32)).astype(BF16)


def kernel(
    tok_hbm, ids_ref, slots_ref, wg_hbm, wu_hbm, wd_hbm, out_hbm,
    xbuf, other, wgu, wd, acc, ps, pr, hid, c1s, c1r, z2s, z2r, z1s, z1r, q0, f0, ys, yr,
    send_sem, recv_sem, local_sem,
):
    XP, XM = device(0, 1, 0, 0, 0), device(0, 3, 0, 0, 0)
    Y2, YN = device(1, 0, 0, 0, 0), device(0, 0, 1, 0, 0)
    ZP, ZM = device(0, 0, 0, 1, 0), device(0, 0, 0, 3, 0)
    CORE = device(0, 0, 0, 0, 1)
    started = []
    left = []

    def send(src, dst, to):
        i = len(started)
        copy = pltpu.make_async_remote_copy(
            src_ref=src, dst_ref=dst, send_sem=send_sem.at[i], recv_sem=recv_sem.at[i],
            device_id=to, device_id_type=MESH,
        )
        copy.start()
        started.append(copy)
        left.append(copy)
        return copy

    def sent(copy):
        copy.wait_send()
        left[:] = [other_copy for other_copy in left if other_copy is not copy]

    tok_loads = {}
    for s in (4, 5, 6, 7, 0, 1, 2, 3):
        load = pltpu.make_async_copy(tok_hbm.at[:, shard_columns(s)], c1r.at[s, pl.ds(0, RUN)], local_sem.at[s])
        load.start()
        tok_loads[s] = load
    own_loads = []
    for k, (src, dst) in enumerate(((wg_hbm, wgu.at[0, 0]), (wu_hbm, wgu.at[1, 0]), (wd_hbm, wd.at[0]))):
        load = pltpu.make_async_copy(src, dst, local_sem.at[8 + k])
        load.start()
        own_loads.append(load)

    barrier = pltpu.get_barrier_semaphore()
    for to in (XP, XM, Y2, YN, ZP, ZM, CORE):
        pl.semaphore_signal(barrier, inc=1, device_id=to, device_id_type=MESH)
    pl.semaphore_wait(barrier, 7)

    g_x = (send(wg_hbm, wgu.at[0, 3], XP), send(wg_hbm, wgu.at[0, 1], XM))
    u_x = (send(wu_hbm, wgu.at[1, 3], XP), send(wu_hbm, wgu.at[1, 1], XM))

    row = lax.broadcasted_iota(jnp.int32, (SLOTS, RUN), 0)
    picker_t = jnp.where(row == slot_row(ids_ref, slots_ref), 1.0, 0.0).astype(BF16)

    def pack(s):
        tok_loads[s].wait()
        return jnp.dot(picker_t, c1r[s, pl.ds(0, RUN), :], preferred_element_type=F32).astype(BF16)

    def block(w, rc, ryl, rz, half=None):
        at = pl.ds(w * ROWS + rz * 256 + rc * 128 + ryl * 64, 64)
        if half is None:
            return xbuf.at[:, at]
        return xbuf.at[pl.ds(half * 2, 2), at]

    to_core = []

    def core(w, ryl, rz, half=None):
        to_core.append(send(block(w, 0, ryl, rz, half), block(w, 1, ryl, rz, half), CORE))

    def spread(w, ryl):
        return (
            send(block(w, 0, ryl, 0), block(w, 0, ryl, 3), ZP),
            send(block(w, 0, ryl, 0), block(w, 0, ryl, 1), ZM),
        )

    def relay(w, ryl, first):
        first[0].wait_recv()
        up = send(block(w, 0, ryl, 3, 0), block(w, 0, ryl, 2, 0), ZP)
        first[1].wait_recv()
        down = send(block(w, 0, ryl, 1, 1), block(w, 0, ryl, 2, 1), ZM)
        core(w, ryl, 3)
        core(w, ryl, 1)
        return up, down

    def land(w, ryl, relays):
        for half in (0, 1):
            relays[half].wait_recv()
            core(w, ryl, 2, half)

    for r in range(4):
        other[r] = pack(4 + r)
    x_2 = send(other, block(1, 0, 0, 0), Y2)
    for r in range(4):
        xbuf[r, pl.ds(0, SLOTS), :] = pack(r)
    x_z0 = spread(0, 0)
    x_y0 = send(block(0, 0, 0, 0), block(0, 0, 1, 0), YN)
    core(0, 0, 0)

    def relay_weight(k, first):
        first[0].wait_recv()
        a = send(wgu.at[k, 3, pl.ds(0, 384)], wgu.at[k, 2, pl.ds(0, 384)], XP)
        first[1].wait_recv()
        return a, send(wgu.at[k, 1, pl.ds(384, 384)], wgu.at[k, 2, pl.ds(384, 384)], XM)

    x_2.wait_recv()
    x_z1 = spread(1, 0)
    x_y1 = send(block(1, 0, 0, 0), block(1, 0, 1, 0), YN)
    d_y = send(wd_hbm, wd.at[4], Y2)
    core(1, 0, 0)
    x_r0 = relay(0, 0, x_z0)
    x_y0.wait_recv()
    x_yz0 = spread(0, 1)
    core(0, 1, 0)
    g_r = relay_weight(0, g_x)
    x_r1 = relay(1, 0, x_z1)
    x_y1.wait_recv()
    x_yz1 = spread(1, 1)
    core(1, 1, 0)
    land(0, 0, x_r0)
    x_yr0 = relay(0, 1, x_yz0)
    land(1, 0, x_r1)
    u_r = relay_weight(1, u_x)
    d_x = (send(wd_hbm, wd.at[3], XP), send(wd_hbm, wd.at[1], XM))
    x_yr1 = relay(1, 1, x_yz1)
    d_y.wait_recv()
    d_p = (send(wd.at[4], wd.at[7], XP), send(wd.at[4], wd.at[5], XM))
    land(0, 1, x_yr0)
    land(1, 1, x_yr1)
    for copy in to_core:
        copy.wait_recv()
    for load in own_loads:
        load.wait()
    for copy in (*g_r, *u_r):
        copy.wait_recv()

    def partial(w, rz, dst, rows):
        @pl.loop(0, 4)
        def _(n):
            k, columns = n // 2, pl.ds(pl.multiple_of((n % 2) * 256, 256), 256)
            total = jnp.dot(xbuf[0, pl.ds(w * ROWS + rz * 256, 256), :], wgu[k, 0, :, columns], preferred_element_type=F32)
            for r in range(1, 4):
                total += jnp.dot(
                    xbuf[r, pl.ds(w * ROWS + rz * 256, 256), :], wgu[k, r, :, columns], preferred_element_type=F32
                )
            dst[rows, pl.ds(pl.multiple_of(n * 256, 256), 256)] = total.astype(dst.dtype)

    p = {}

    def partial_out(rz):
        partial(1, rz, ps.at[rz], pl.ds(0, 256))
        for rc in (1, 0):
            at = pl.ds(rc * 128, 128)
            p[rz, rc] = send(ps.at[rz, at], pr.at[rz, at], Y2)

    def partial_own(rz):
        partial(0, rz, acc, pl.ds(rz * 256, 256))

    def hidden(rz, rc):
        p[rz, rc].wait_recv()
        rows, at = pl.ds(rz * 256 + rc * 128, 128), pl.ds(rc * 128, 128)
        gate = acc[rows, 0:UNITS] + pr[rz, at, 0:UNITS].astype(F32)
        up = acc[rows, UNITS:] + pr[rz, at, UNITS:].astype(F32)
        hid[rows, :] = (gate / (1.0 + jnp.exp(-gate)) * up).astype(BF16)

    c1, z2, z1, y1, outs = {}, {}, {}, {}, {}
    core_order = []

    def down(rz, rc, s):
        return jnp.dot(hid[pl.ds(rz * 256 + rc * 128, 128), :], wd[s], preferred_element_type=F32)

    def to_sibling(rz, *shards):
        for s in shards:
            i = len(core_order)
            if i >= CORE_SENDS:
                sent(core_order[i - CORE_SENDS])
            c1s[i % CORE_SENDS] = down(rz, 1, s).astype(BF16)
            c1[rz, s] = send(c1s.at[i % CORE_SENDS], c1r.at[s, pl.ds(rz * 128, 128)], CORE)
            core_order.append(c1[rz, s])

    def sums(rz, *shards):
        for s in shards:
            c1[rz, s].wait_recv()
            total = down(rz, 0, s) + c1r[s, pl.ds(rz * 128, 128), :].astype(F32)
            if rz == 0:
                q0[s] = total
            elif rz == 2:
                z2s[s, 0] = total[:, 0:384].astype(BF16)
                z2s[s, 1] = total[:, 384:768].astype(BF16)
                z2[s] = (send(z2s.at[s, 0], z2r.at[s, 0], ZP), send(z2s.at[s, 1], z2r.at[s, 1], ZM))
            elif rz == 1:
                z2[s][0].wait_recv()
                z1s[s, 0, :, 0:384] = (total[:, 0:384] + z2r[s, 0].astype(F32)).astype(BF16)
                z1s[s, 0, :, 384:768] = total[:, 384:768].astype(BF16)
                z1[s, 0] = send(z1s.at[s, 0], z1r.at[s, 0], ZP)
            else:
                z2[s][1].wait_recv()
                z1s[s, 1, :, 0:384] = total[:, 0:384].astype(BF16)
                z1s[s, 1, :, 384:768] = (total[:, 384:768] + z2r[s, 1].astype(F32)).astype(BF16)
                z1[s, 1] = send(z1s.at[s, 1], z1r.at[s, 1], ZM)

    def to_y(*shards):
        for s in shards:
            z1[s, 0].wait_recv()
            z1[s, 1].wait_recv()
            total = q0[s] + z1r[s, 0].astype(F32) + z1r[s, 1].astype(F32)
            f0[s] = total[0:64]
            ys[s] = total[64:128].astype(BF16)
            y1[s] = send(ys.at[s], yr.at[s], YN)

    def rows_out(*shards):
        for s in shards:
            y1[s].wait_recv()
            f0[s] += yr[s].astype(F32)
            outs[s] = pltpu.make_async_copy(f0.at[s], out_hbm.at[:, shard_columns(s)], local_sem.at[11 + s])
            outs[s].start()

    def relay_down(first, near, far, opposite):
        first[0].wait_recv()
        a = send(wd.at[near, pl.ds(0, 256)], wd.at[far, pl.ds(0, 256)], XP)
        first[1].wait_recv()
        return a, send(wd.at[opposite, pl.ds(256, 256)], wd.at[far, pl.ds(256, 256)], XM)

    partial_out(2)
    partial_out(1)
    partial_own(2)
    partial_out(3)
    partial_out(0)
    hidden(2, 1)
    to_sibling(2, 0, 4)
    partial_own(1)
    hidden(2, 0)
    sums(2, 0, 4)
    d_r = relay_down(d_x, 3, 2, 1)
    to_sibling(2, 1, 3)
    sums(2, 1, 3)
    partial_own(3)
    hidden(1, 1)
    to_sibling(1, 0, 4, 1, 3)
    partial_own(0)
    hidden(1, 0)
    sums(1, 0, 4, 1, 3)
    d_pr = relay_down(d_p, 7, 6, 5)
    to_sibling(2, 5, 7)
    sums(2, 5, 7)
    hidden(3, 1)
    to_sibling(3, 0, 4, 1, 3)
    hidden(3, 0)
    sums(3, 0, 4, 1, 3)
    to_sibling(1, 5, 7)
    to_sibling(3, 5, 7)
    sums(1, 5, 7)
    sums(3, 5, 7)
    d_r[0].wait_recv()
    d_r[1].wait_recv()
    to_sibling(2, 2)
    hidden(0, 1)
    sums(2, 2)
    to_sibling(0, 0, 4, 1, 3)
    to_sibling(1, 2)
    to_sibling(3, 2)
    hidden(0, 0)
    sums(1, 2)
    sums(3, 2)
    d_pr[0].wait_recv()
    d_pr[1].wait_recv()
    to_sibling(2, 6)
    sums(0, 0, 4)
    sums(2, 6)
    to_sibling(1, 6)
    to_sibling(3, 6)
    sums(0, 1, 3)
    to_y(0, 4, 1)
    sums(1, 6)
    sums(3, 6)
    to_y(3)
    to_sibling(0, 5, 7, 2, 6)
    sums(0, 5, 7, 2, 6)
    rows_out(0, 4, 1, 3)
    to_y(5, 7)
    to_y(2)
    rows_out(5, 7)
    to_y(6)
    rows_out(2, 6)

    for copy in outs.values():
        copy.wait()
    for copy in list(left):
        copy.wait_send()


def body(tokens, expert_ids, slot_ids, gate_probs, gate_weight, up_weight, down_weight):
    hbm, vmem = pl.BlockSpec(memory_space=pl.ANY), pl.BlockSpec(memory_space=pltpu.VMEM)
    ids, slots, probs = expert_ids.T, slot_ids.T, gate_probs.T
    rows = pl.pallas_call(
        kernel,
        out_shape=jax.ShapeDtypeStruct((SLOTS, tokens.shape[1]), F32),
        in_specs=[hbm, vmem, vmem, hbm, hbm, hbm],
        out_specs=hbm,
        scratch_shapes=[
            pltpu.VMEM((4, 2 * ROWS, DEPTH), BF16),
            pltpu.VMEM((4, SLOTS, DEPTH), BF16),
            pltpu.VMEM((2, 4, DEPTH, UNITS), BF16),
            pltpu.VMEM((SHARDS, UNITS, DEPTH), BF16),
            pltpu.VMEM((ROWS, 2 * UNITS), F32),
            pltpu.VMEM((4, 256, 2 * UNITS), BF16),
            pltpu.VMEM((4, 256, 2 * UNITS), BF16),
            pltpu.VMEM((ROWS, UNITS), BF16),
            pltpu.VMEM((CORE_SENDS, 128, DEPTH), BF16),
            pltpu.VMEM((SHARDS, 512, DEPTH), BF16),
            pltpu.VMEM((SHARDS, 2, 128, 384), BF16),
            pltpu.VMEM((SHARDS, 2, 128, 384), BF16),
            pltpu.VMEM((SHARDS, 2, 128, DEPTH), BF16),
            pltpu.VMEM((SHARDS, 2, 128, DEPTH), BF16),
            pltpu.VMEM((SHARDS, 128, DEPTH), F32),
            pltpu.VMEM((SHARDS, SLOTS, DEPTH), F32),
            pltpu.VMEM((SHARDS, SLOTS, DEPTH), BF16),
            pltpu.VMEM((SHARDS, SLOTS, DEPTH), BF16),
            pltpu.SemaphoreType.DMA((COPIES,)),
            pltpu.SemaphoreType.DMA((COPIES,)),
            pltpu.SemaphoreType.DMA((20,)),
        ],
        compiler_params=pltpu.CompilerParams(
            collective_id=0, has_side_effects=True, vmem_limit_bytes=62 << 20
        ),
        cost_estimate=pl.CostEstimate(flops=20_000_000_000, bytes_accessed=60_000_000, transcendentals=1_000_000),
    )(tokens, ids, slots, gate_weight, up_weight, down_weight)
    whole = pl.BlockSpec((2, RUN), lambda i: (0, 0))
    return pl.pallas_call(
        combine,
        grid=(4,),
        out_shape=jax.ShapeDtypeStruct(tokens.shape, BF16),
        in_specs=[whole, whole, whole, pl.BlockSpec((SLOTS, 2 * DEPTH), lambda i: (0, i))],
        out_specs=pl.BlockSpec((RUN, 2 * DEPTH), lambda i: (0, i)),
    )(ids, slots, probs, rows)


def solution(mesh):
    return jax.shard_map(
        body,
        mesh=mesh,
        in_specs=(
            P(("dp", "tensor"), None),
            P(("dp", "tensor"), None),
            P(("dp", "tensor"), None),
            P(("dp", "tensor"), None),
            P("dp", "tensor"),
            P("dp", "tensor"),
            P("tensor", "dp"),
        ),
        out_specs=P(("dp", "tensor"), None),
        check_vma=False,
    )
```

time: 471 us -> 161 us (0.34)
  waiting for transfers between devices: 413 us -> 0 us
  Pallas kernels: 0 us -> 161 us
  matrix products: 42 us -> 0 us
  between operations: 13.2 us -> 0.01 us
    all_gather x4 -> x0, waiting for transfers between devices: 331 us -> none  [the longest x1 90 us: body(): lax.all_gather(gate_weight, 'dp', axis=0, tiled=True)]
    pallas_call x0 -> x2, Pallas kernels: none -> 161 us  [the longest x1 157 us: body(): pl.pallas_call(kernel, out_shape=jax.ShapeDtypeStruct((SLOTS, tokens.shap...]
    reduce_scatter x1 -> x0, waiting for transfers between devices: 80.1 us -> none  [body(): lax.psum_scatter(term_rows.astype(jnp.bfloat16), 'tensor', scatter_dimens...]
    dot_general x4 -> x0, matrix products: 42 us -> none  [the longest x1 22.9 us: body(): jnp.dot(hidden, lax.all_gather(down_weight, 'dp', axis=1, tiled=True), pr...]
  transfers between devices with their start and end apart: 5 -> 0, of which waited for: 5 -> 0; matrix products, arithmetic and copies ran while one was open for 3% -> 0% of each run, Pallas kernels for 0% -> 0%
where the time goes in v3:
time: 161 us
  Pallas kernels  161 us (100%)
    pallas_call x1, Pallas kernels, body(): pl.pallas_call(kernel, out_shape=jax.ShapeDtypeStruct((SLOTS, tokens.shap...  157 us
    pallas_call x1, Pallas kernels, body(): pl.pallas_call(combine, grid=(4,), out_shape=jax.ShapeDtypeStruct(tokens....  4.66 us

profile of v3, /device:TPU:0, one launch (start us, length us, event | category | flops | bytes accessed | tf_op | source)
XLA Modules:
  0.0 161.2 jit_solution(5802189741508321049)
XLA Ops:
  0.0 156.5 %shard_map.73.rows_ref = f32[64,6144]{1,0:T(8,128)} custom-call(bf16[256,6144]{1,0:T(8,128)(2,1)} %tok_hbm.1, s32[2,256]{1,0:T(2,128)} %bitcast.3, s32[2,256]{1,0:T(2,128)} %bitcast.5, bf16[768,512]{1,0:T(8,128)(2,1)} %wg_hbm.1, bf16[768,512]{1,0:T(8,128)(2,1)} %wu_hbm.1, bf16[512,768]{1,0:T(8,128)(2,1)} %wd_hbm.1), custom_call_target="tpu_custom_call" | custom-call | flops 20000000000 | bytes 60000000 | tf_op jit(solution)/shard_map/pallas_call | solution.py:349
  156.5 4.7 %shard_map.74 = bf16[256,6144]{1,0:T(8,128)(2,1)} custom-call(s32[2,256]{1,0:T(2,128)} %bitcast.4, s32[2,256]{1,0:T(2,128)} %bitcast.6, f32[2,256]{1,0:T(2,128)} %bitcast.7, f32[64,6144]{1,0:T(8,128)} %shard_map.73.rows_ref), custom_call_target="tpu_custom_call" | custom-call | tf_op jit(solution)/shard_map/pallas_call | solution.py:383

commit v4 on v0

v4 whole, which is shorter than its diff:
```python
import functools

import jax
import jax.numpy as jnp
from jax import lax
from jax.experimental import pallas as pl
from jax.experimental.pallas import tpu as pltpu
from jax.sharding import PartitionSpec as P

MESH = pl.DeviceIdType.MESH
F32 = jnp.float32
BF16 = jnp.bfloat16

SLOTS = 64
RUN = 256
DEPTH = 768
UNITS = 512
ROWS = 1024
SHARDS = 8
COPIES = 176
KEPT = 16

ORDER = (0, 4, 1, 3, 5, 7, 2, 6)
Y_FIRST = 7


def place():
    dp, tensor = lax.axis_index("dp"), lax.axis_index("tensor")
    return dp // 4, dp % 4, tensor // 8, (tensor // 2) % 4, tensor % 2


def device(d_yh, d_x, d_yl, d_z, d_c):
    yh, x, yl, z, c = place()
    yh, x, yl, z, c = (yh + d_yh) % 2, (x + d_x) % 4, (yl + d_yl) % 2, (z + d_z) % 4, (c + d_c) % 2
    return (yh * 4 + x, yl * 8 + z * 2 + c)


def shard_columns(s):
    yh, x, _, _, _ = place()
    owner = ((yh + s // 4) % 2) * 4 + (x + s % 4) % 4
    return pl.ds(pl.multiple_of(owner * DEPTH, DEPTH), DEPTH)


def slot_row(ids_ref, slots_ref):
    first = jnp.where(ids_ref[0:1, :] == 0, slots_ref[0:1, :], SLOTS)
    return jnp.minimum(first, jnp.where(ids_ref[1:2, :] == 0, slots_ref[1:2, :], SLOTS))


def combine(picker_ref, weight_ref, rows_ref, mixed_ref):
    mixed = jnp.dot(picker_ref[...], rows_ref[...], preferred_element_type=F32)
    mixed_ref[...] = (weight_ref[:, 0:1] * mixed).astype(BF16)


def kernel(
    tok_hbm, ids_ref, slots_ref, probs_ref, wg_hbm, wu_hbm, wd_hbm, out_hbm, picker_ref, weight_ref,
    xbuf, other, wgu, wd, acc, ps, pr, hid, c1s, keep, c1r, z2s, z2r, z1s, z1r, q0, ys, yr,
    send_sem, recv_sem, local_sem,
):
    XP, XM = device(0, 1, 0, 0, 0), device(0, 3, 0, 0, 0)
    Y2, YN = device(1, 0, 0, 0, 0), device(0, 0, 1, 0, 0)
    ZP, ZM = device(0, 0, 0, 1, 0), device(0, 0, 0, 3, 0)
    CORE = device(0, 0, 0, 0, 1)
    started, left, here = [], {}, set()

    def send(src, dst, to):
        i = len(started)
        copy = pltpu.make_async_remote_copy(
            src_ref=src, dst_ref=dst, send_sem=send_sem.at[i], recv_sem=recv_sem.at[i],
            device_id=to, device_id_type=MESH,
        )
        copy.start()
        started.append(copy)
        left[i] = copy
        return i

    def arrived(*copies):
        for i in copies:
            if i not in here:
                started[i].wait_recv()
                here.add(i)

    def sent(i):
        if i in left:
            left.pop(i).wait_send()

    tok_loads = {}
    for s in (4, 5, 6, 7, 0, 1, 2, 3):
        load = pltpu.make_async_copy(tok_hbm.at[:, shard_columns(s)], c1r.at[s, pl.ds(0, RUN)], local_sem.at[s])
        load.start()
        tok_loads[s] = load
    own_loads = []
    half = (pl.ds(0, 256), pl.ds(256, 256))
    for h in (0, 1):
        for k, src in enumerate((wg_hbm, wu_hbm)):
            own_loads.append(
                pltpu.make_async_copy(src.at[:, half[h]], wgu.at[h, 0, :, half[k]], local_sem.at[8 + 2 * h + k])
            )
    own_loads.append(pltpu.make_async_copy(wd_hbm, wd.at[0], local_sem.at[12]))
    for load in own_loads:
        load.start()

    barrier = pltpu.get_barrier_semaphore()
    for to in (XP, XM, Y2, YN, ZP, ZM, CORE):
        pl.semaphore_signal(barrier, inc=1, device_id=to, device_id_type=MESH)
    pl.semaphore_wait(barrier, 7)

    w_x = {}
    for h in (0, 1):
        for k, src in enumerate((wg_hbm, wu_hbm)):
            w_x[h, k] = (
                send(src.at[:, half[h]], wgu.at[h, 3, :, half[k]], XP),
                send(src.at[:, half[h]], wgu.at[h, 1, :, half[k]], XM),
            )

    row = lax.broadcasted_iota(jnp.int32, (SLOTS, RUN), 0)
    picker_t = jnp.where(row == slot_row(ids_ref, slots_ref), 1.0, 0.0).astype(BF16)

    def pack(s):
        tok_loads[s].wait()
        return jnp.dot(picker_t, c1r[s, pl.ds(0, RUN), :], preferred_element_type=F32).astype(BF16)

    def block(w, rc, ryl, rz, part=None):
        at = pl.ds(w * ROWS + rz * 256 + ryl * 128 + rc * 64, 64)
        if part is None:
            return xbuf.at[:, at]
        return xbuf.at[pl.ds(part * 2, 2), at]

    from_core = {}

    def core(w, ryl, rz, part=None):
        copy = send(block(w, 0, ryl, rz, part), block(w, 1, ryl, rz, part), CORE)
        from_core.setdefault((w, rz), []).append(copy)

    def spread(w, ryl):
        return (
            send(block(w, 0, ryl, 0), block(w, 0, ryl, 3), ZP),
            send(block(w, 0, ryl, 0), block(w, 0, ryl, 1), ZM),
        )

    def relay(w, ryl, first):
        arrived(first[0])
        up = send(block(w, 0, ryl, 3, 0), block(w, 0, ryl, 2, 0), ZP)
        arrived(first[1])
        return up, send(block(w, 0, ryl, 1, 1), block(w, 0, ryl, 2, 1), ZM)

    def both_cores(w, ryl, first):
        arrived(*first)
        core(w, ryl, 3)
        core(w, ryl, 1)

    def land(w, ryl, relays):
        for part in (0, 1):
            arrived(relays[part])
            core(w, ryl, 2, part)

    for r in range(4):
        other[r] = pack(4 + r)
    x_2 = send(other, block(1, 0, 0, 0), Y2)
    for r in range(4):
        xbuf[r, pl.ds(0, SLOTS), :] = pack(r)
    x_z0 = spread(0, 0)
    x_y0 = send(block(0, 0, 0, 0), block(0, 0, 1, 0), YN)
    core(0, 0, 0)

    upper, lower = pl.ds(0, 384), pl.ds(384, 384)

    def relay_weight(h):
        copies = []
        for k in (0, 1):
            arrived(w_x[h, k][0])
            copies.append(send(wgu.at[h, 3, upper, half[k]], wgu.at[h, 2, upper, half[k]], XP))
            arrived(w_x[h, k][1])
            copies.append(send(wgu.at[h, 1, lower, half[k]], wgu.at[h, 2, lower, half[k]], XM))
        return copies

    def partial(w, rz, h, dst, rows, shards=(0, 1, 3, 2), more=False):
        arrived(*from_core[w, rz])
        if 2 in shards:
            arrived(*(w_r0, w_r1)[h])

        @pl.loop(0, 2)
        def _(n):
            columns = pl.ds(pl.multiple_of(n * 256, 256), 256)
            at = pl.ds(w * ROWS + rz * 256, 256)
            into = pl.ds(pl.multiple_of(h * 512 + n * 256, 256), 256)
            total = dst[rows, into] if more else None
            for r in shards:
                part = jnp.dot(xbuf[r, at, :], wgu[h, r, :, columns], preferred_element_type=F32)
                total = part if total is None else total + part
            dst[rows, into] = total.astype(dst.dtype)

    def partial_out(rz, h):
        partial(1, rz, h, ps.at[rz], pl.ds(0, 256))

    def partial_own(rz, **kind):
        for h in (0, 1):
            partial(0, rz, h, acc, pl.ds(rz * 256, 256), **kind)

    def partial_last(rz):
        partial_own(rz, shards=(2,), more=True)

    row = lax.broadcasted_iota(jnp.int32, (2 * SLOTS, RUN), 0)
    picked = jnp.where(row >= SLOTS, row - SLOTS, row) == slot_row(ids_ref, slots_ref)
    weight = jnp.where(ids_ref[0:1, :] == 0, probs_ref[0:1, :], 0.0)
    weight += jnp.where(ids_ref[1:2, :] == 0, probs_ref[1:2, :], 0.0)
    picker_ref[...] = jnp.where(picked, 1.0, 0.0).T.astype(BF16)
    weight = jnp.sum(jnp.where(picked, weight, 0.0).T[:, :SLOTS], axis=1, keepdims=True)
    weight_ref[...] = jnp.broadcast_to(weight, (RUN, 2 * SLOTS))

    arrived(x_2)
    x_z1 = spread(1, 0)
    x_y1 = send(block(1, 0, 0, 0), block(1, 0, 1, 0), YN)
    d_y = send(wd_hbm, wd.at[4], Y2)
    core(1, 0, 0)
    both_cores(0, 0, x_z0)
    arrived(x_y0)
    x_yz0 = spread(0, 1)
    core(0, 1, 0)
    x_r1 = relay(1, 0, x_z1)
    both_cores(1, 0, x_z1)
    w_r0 = relay_weight(0)
    arrived(x_y1)
    x_yz1 = spread(1, 1)
    core(1, 1, 0)
    both_cores(0, 1, x_yz0)
    land(1, 0, x_r1)
    w_r1 = relay_weight(1)
    d_x = (send(wd_hbm, wd.at[3], XP), send(wd_hbm, wd.at[1], XM))
    for load in own_loads:
        load.wait()
    partial_own(0, shards=(0, 1, 3))
    partial_own(1, shards=(0, 1, 3))
    partial_own(3, shards=(0, 1, 3))
    x_yr1 = relay(1, 1, x_yz1)
    x_r0 = relay(0, 0, x_z0)
    x_yr0 = relay(0, 1, x_yz0)
    both_cores(1, 1, x_yz1)
    arrived(d_y)
    d_p = (send(wd.at[4], wd.at[7], XP), send(wd.at[4], wd.at[5], XM))
    partial_out(0, 0)
    land(1, 1, x_yr1)
    partial_out(1, 0)

    p = {(rz, ryl): [] for rz in range(4) for ryl in (0, 1)}

    def exchange(rz, ryl):
        at = pl.ds(ryl * 128, 128)
        p[rz, ryl].append(send(ps.at[rz, at], pr.at[rz, at], Y2))

    def hidden(rz, ryl):
        arrived(*p[rz, ryl])
        rows, at = pl.ds(rz * 256 + ryl * 128, 128), pl.ds(ryl * 128, 128)
        for h in (0, 1):
            g, u = pl.ds(h * 512, 256), pl.ds(h * 512 + 256, 256)
            gate = acc[rows, g] + pr[rz, at, g].astype(F32)
            up = acc[rows, u] + pr[rz, at, u].astype(F32)
            hid[rows, half[h]] = (gate / (1.0 + jnp.exp(-gate)) * up).astype(BF16)

    c1, z2, z1, y1, outs = {}, {}, {}, {}, {}
    slots, busy = [], set()

    def down(rz, ryl, first, count):
        if len(slots) % KEPT + count > KEPT:
            slots.extend([None] * (KEPT - len(slots) % KEPT))
        start = len(slots) % KEPT
        for j in range(count):
            if len(slots) + j >= KEPT and slots[len(slots) + j - KEPT] is not None:
                sent(slots[len(slots) + j - KEPT])
        assert busy.isdisjoint(range(start, start + count))
        busy.update(range(start, start + count))
        rows = pl.ds(rz * 256 + ryl * 128, 128)
        for j in range(count):
            part = jnp.dot(hid[rows, :], wd[ORDER[first + j]], preferred_element_type=F32)
            keep[start + j] = part[0:64]
            c1s[pl.ds((start + j) * 64, 64), :] = part[64:128].astype(BF16)
        copy = send(
            c1s.at[pl.ds(start * 64, count * 64)], c1r.at[rz * 2 + ryl, pl.ds(first * 64, count * 64)], CORE
        )
        slots.extend([copy] * count)
        c1[rz, ryl, first] = (copy, start, count)

    def sums(rz, ryl, first):
        copy, start, count = c1[rz, ryl, first]
        arrived(copy)
        for j in range(count):
            t = first + j
            total = keep[start + j] + c1r[rz * 2 + ryl, pl.ds(t * 64, 64), :].astype(F32)
            if t >= Y_FIRST:
                spot = Y_FIRST + (t - Y_FIRST) * 4 + rz
                if ryl == 1:
                    ys[spot] = total.astype(BF16)
                    y1[t, rz] = send(ys.at[spot], yr.at[spot], YN)
                    continue
                arrived(y1[t, rz])
                total += yr[spot].astype(F32)
            if rz == 0:
                q0[ryl, t] = total
            elif rz == 2:
                z2s[ryl, 0, t] = total[:, 0:384].astype(BF16)
                z2s[ryl, 1, t] = total[:, 384:768].astype(BF16)
            elif rz == 1:
                arrived(z2[ryl, 0, t])
                z1s[ryl, 0, t, :, 0:384] = (total[:, 0:384] + z2r[ryl, 0, t].astype(F32)).astype(BF16)
                z1s[ryl, 0, t, :, 384:768] = total[:, 384:768].astype(BF16)
            else:
                arrived(z2[ryl, 1, t])
                z1s[ryl, 1, t, :, 0:384] = total[:, 0:384].astype(BF16)
                z1s[ryl, 1, t, :, 384:768] = (total[:, 384:768] + z2r[ryl, 1, t].astype(F32)).astype(BF16)
        busy.difference_update(range(start, start + count))
        if first >= Y_FIRST and ryl == 1:
            return
        group = pl.ds(first, count)
        for way, to in ((0, ZP), (1, ZM)):
            if rz == 2:
                copy = send(z2s.at[ryl, way, group], z2r.at[ryl, way, group], to)
                for j in range(count):
                    z2[ryl, way, first + j] = copy
            elif rz == (1, 3)[way]:
                copy = send(z1s.at[ryl, way, group], z1r.at[ryl, way, group], to)
                for j in range(count):
                    z1[ryl, way, first + j] = copy

    def both(rz, ryl, first, count):
        down(rz, ryl, first, count)
        sums(rz, ryl, first)

    def over_z(ryl, t):
        arrived(z1[ryl, 0, t], z1[ryl, 1, t])
        return q0[ryl, t] + z1r[ryl, 0, t].astype(F32) + z1r[ryl, 1, t].astype(F32)

    def to_y(first, count):
        for t in range(first, first + count):
            ys[t] = over_z(1, t).astype(BF16)
        group = pl.ds(first, count)
        copy = send(ys.at[group], yr.at[group], YN)
        for t in range(first, first + count):
            y1[t] = copy

    def rows_out(first, count):
        for t in range(first, first + count):
            total = over_z(0, t)
            if t < Y_FIRST:
                arrived(y1[t])
                total += yr[t].astype(F32)
            head = total.astype(BF16)
            z1r[0, 0, t] = head
            z1r[0, 1, t] = (total - head.astype(F32)).astype(BF16)
            for part in (0, 1):
                outs[t, part] = pltpu.make_async_copy(
                    z1r.at[0, part, t],
                    out_hbm.at[pl.ds(part * SLOTS, SLOTS), shard_columns(ORDER[t])],
                    local_sem.at[13 + 2 * t + part],
                )
                outs[t, part].start()

    def relay_down(first, near, far, opposite):
        arrived(first[0])
        a = send(wd.at[near, half[0]], wd.at[far, half[0]], XP)
        arrived(first[1])
        return a, send(wd.at[opposite, half[1]], wd.at[far, half[1]], XM)

    partial_out(2, 0)
    early = send(ps.at[2, :, pl.ds(0, 512)], pr.at[2, :, pl.ds(0, 512)], Y2)
    land(0, 0, x_r0)
    land(0, 1, x_yr0)
    partial_out(3, 0)
    partial_out(2, 1)
    for ryl in (1, 0):
        at = pl.ds(ryl * 128, 128), pl.ds(512, 512)
        p[2, ryl] += [early, send(ps.at[2, at[0], at[1]], pr.at[2, at[0], at[1]], Y2)]
    partial_out(1, 1)
    exchange(1, 1)
    partial_out(3, 1)
    exchange(3, 1)
    exchange(1, 0)
    exchange(3, 0)
    partial_own(2)
    hidden(2, 1)
    down(2, 1, 0, 2)
    partial_last(1)
    sums(2, 1, 0)
    hidden(2, 0)
    down(2, 0, 0, 2)
    partial_out(0, 1)
    exchange(0, 1)
    exchange(0, 0)
    sums(2, 0, 0)
    hidden(1, 1)
    down(1, 1, 0, 2)
    d_r = relay_down(d_x, 3, 2, 1)
    down(2, 1, 2, 2)
    down(2, 0, 2, 2)
    sums(1, 1, 0)
    sums(2, 1, 2)
    sums(2, 0, 2)
    down(1, 1, 2, 2)
    partial_last(3)
    sums(1, 1, 2)
    hidden(3, 1)
    down(3, 1, 0, 4)
    partial_last(0)
    sums(3, 1, 0)
    hidden(1, 0)
    down(1, 0, 0, 4)
    sums(1, 0, 0)
    hidden(3, 0)
    down(3, 0, 0, 4)
    d_pr = relay_down(d_p, 7, 6, 5)
    down(2, 1, 4, 2)
    down(2, 0, 4, 2)
    sums(2, 1, 4)
    sums(2, 0, 4)
    sums(3, 0, 0)
    hidden(0, 1)
    down(0, 1, 0, 4)
    down(1, 1, 4, 2)
    down(3, 1, 4, 2)
    sums(0, 1, 0)
    sums(1, 1, 4)
    sums(3, 1, 4)
    down(1, 0, 4, 2)
    down(3, 0, 4, 2)
    to_y(0, 4)
    sums(1, 0, 4)
    sums(3, 0, 4)
    arrived(*d_r)
    down(2, 1, 6, 1)
    down(2, 0, 6, 1)
    hidden(0, 0)
    down(0, 0, 0, 4)
    sums(2, 1, 6)
    sums(2, 0, 6)
    down(0, 1, 4, 2)
    sums(0, 0, 0)
    down(0, 0, 4, 2)
    sums(0, 1, 4)
    sums(0, 0, 4)
    for rz, ryl in ((1, 1), (3, 1), (1, 0), (3, 0), (0, 1), (0, 0)):
        down(rz, ryl, 6, 1)
    sums(0, 1, 6)
    sums(0, 0, 6)
    arrived(*d_pr)
    for rz in (2, 3, 1, 0):
        down(rz, 1, 7, 1)
    for rz in (2, 3, 1, 0):
        sums(rz, 1, 7)
    for rz, ryl in ((1, 1), (3, 1), (1, 0), (3, 0)):
        sums(rz, ryl, 6)
    for rz in (2, 3, 1, 0):
        down(rz, 0, 7, 1)
    sums(2, 0, 7)
    to_y(4, 2)
    sums(3, 0, 7)
    sums(1, 0, 7)
    sums(0, 0, 7)
    rows_out(0, 4)
    to_y(6, 1)
    rows_out(4, 2)
    rows_out(7, 1)
    rows_out(6, 1)

    for copy in outs.values():
        copy.wait()
    for copy in left.values():
        copy.wait_send()
    assert len(started) <= COPIES


def body(tokens, expert_ids, slot_ids, gate_probs, gate_weight, up_weight, down_weight):
    hbm, vmem = pl.BlockSpec(memory_space=pl.ANY), pl.BlockSpec(memory_space=pltpu.VMEM)
    ids, slots, probs = expert_ids.T, slot_ids.T, gate_probs.T
    rows, picker, weight = pl.pallas_call(
        kernel,
        out_shape=(
            jax.ShapeDtypeStruct((2 * SLOTS, tokens.shape[1]), BF16),
            jax.ShapeDtypeStruct((RUN, 2 * SLOTS), BF16),
            jax.ShapeDtypeStruct((RUN, 2 * SLOTS), F32),
        ),
        in_specs=[hbm, vmem, vmem, vmem, hbm, hbm, hbm],
        out_specs=(hbm, vmem, vmem),
        scratch_shapes=[
            pltpu.VMEM((4, 2 * ROWS, DEPTH), BF16),
            pltpu.VMEM((4, SLOTS, DEPTH), BF16),
            pltpu.VMEM((2, 4, DEPTH, UNITS), BF16),
            pltpu.VMEM((SHARDS, UNITS, DEPTH), BF16),
            pltpu.VMEM((ROWS, 2 * UNITS), F32),
            pltpu.VMEM((4, 256, 2 * UNITS), BF16),
            pltpu.VMEM((4, 256, 2 * UNITS), BF16),
            pltpu.VMEM((ROWS, UNITS), BF16),
            pltpu.VMEM((KEPT * 64, DEPTH), BF16),
            pltpu.VMEM((KEPT, 64, DEPTH), F32),
            pltpu.VMEM((8, SHARDS * 64, DEPTH), BF16),
            pltpu.VMEM((2, 2, SHARDS, 64, 384), BF16),
            pltpu.VMEM((2, 2, SHARDS, 64, 384), BF16),
            pltpu.VMEM((2, 2, SHARDS, 64, DEPTH), BF16),
            pltpu.VMEM((2, 2, SHARDS, 64, DEPTH), BF16),
            pltpu.VMEM((2, SHARDS, 64, DEPTH), F32),
            pltpu.VMEM((Y_FIRST + (SHARDS - Y_FIRST) * 4, SLOTS, DEPTH), BF16),
            pltpu.VMEM((Y_FIRST + (SHARDS - Y_FIRST) * 4, SLOTS, DEPTH), BF16),
            pltpu.SemaphoreType.DMA((COPIES,)),
            pltpu.SemaphoreType.DMA((COPIES,)),
            pltpu.SemaphoreType.DMA((29,)),
        ],
        compiler_params=pltpu.CompilerParams(
            collective_id=0, has_side_effects=True, vmem_limit_bytes=62 << 20
        ),
        cost_estimate=pl.CostEstimate(flops=20_000_000_000, bytes_accessed=60_000_000, transcendentals=1_000_000),
    )(tokens, ids, slots, probs, gate_weight, up_weight, down_weight)
    small = pl.BlockSpec((RUN, 2 * SLOTS), lambda i: (0, 0))
    return pl.pallas_call(
        combine,
        grid=(2,),
        out_shape=jax.ShapeDtypeStruct(tokens.shape, BF16),
        in_specs=[small, small, pl.BlockSpec((2 * SLOTS, 4 * DEPTH), lambda i: (0, i))],
        out_specs=pl.BlockSpec((RUN, 4 * DEPTH), lambda i: (0, i)),
    )(picker, weight, rows)


def solution(mesh):
    return jax.shard_map(
        body,
        mesh=mesh,
        in_specs=(
            P(("dp", "tensor"), None),
            P(("dp", "tensor"), None),
            P(("dp", "tensor"), None),
            P(("dp", "tensor"), None),
            P("dp", "tensor"),
            P("dp", "tensor"),
            P("tensor", "dp"),
        ),
        out_specs=P(("dp", "tensor"), None),
        check_vma=False,
    )
```

time: 471 us -> 146 us (0.31)
  waiting for transfers between devices: 413 us -> 0 us
  Pallas kernels: 0 us -> 145 us
  matrix products: 42 us -> 0 us
  between operations: 13.2 us -> 0.01 us
    all_gather x4 -> x0, waiting for transfers between devices: 331 us -> none  [the longest x1 90 us: body(): lax.all_gather(gate_weight, 'dp', axis=0, tiled=True)]
    pallas_call x0 -> x2, Pallas kernels: none -> 145 us  [the longest x1 142 us: body(): pl.pallas_call(kernel, out_shape=(jax.ShapeDtypeStruct((2 * SLOTS, tokens...]
    reduce_scatter x1 -> x0, waiting for transfers between devices: 80.1 us -> none  [body(): lax.psum_scatter(term_rows.astype(jnp.bfloat16), 'tensor', scatter_dimens...]
    dot_general x4 -> x0, matrix products: 42 us -> none  [the longest x1 22.9 us: body(): jnp.dot(hidden, lax.all_gather(down_weight, 'dp', axis=1, tiled=True), pr...]
  transfers between devices with their start and end apart: 5 -> 0, of which waited for: 5 -> 0; matrix products, arithmetic and copies ran while one was open for 3% -> 0% of each run, Pallas kernels for 0% -> 0%
where the time goes in v4:
time: 146 us; the launch traced here: 145 us
  Pallas kernels  145 us (99%)
    pallas_call x1, Pallas kernels, body(): pl.pallas_call(kernel, out_shape=(jax.ShapeDtypeStruct((2 * SLOTS, tokens...  142 us
    pallas_call x1, Pallas kernels, body(): pl.pallas_call(combine, grid=(2,), out_shape=jax.ShapeDtypeStruct(tokens....  3.44 us

profile of v4, /device:TPU:0, one launch (start us, length us, event | category | flops | bytes accessed | tf_op | source)
XLA Modules:
  0.0 145.5 jit_solution(3603107863957075968)
XLA Ops:
  0.0 142.0 %shard_map.73 = (bf16[128,6144]{1,0:T(8,128)(2,1)}, bf16[256,128]{1,0:T(8,128)(2,1)}, f32[256,128]{1,0:T(8,128)}) custom-call(bf16[256,6144]{1,0:T(8,128)(2,1)} %tok_hbm.1, s32[2,256]{1,0:T(2,128)} %bitcast.3, s32[2,256]{1,0:T(2,128)} %bitcast.4, f32[2,256]{1,0:T(2,128)} %bitcast.5, bf16[768,512]{1,0:T(8,128)(2,1)} %wg_hbm.1, bf16[768,512]{1,0:T(8,128)(2,1)} %wu_hbm.1, ...), custom_call_target="tpu_custom_call" | custom-call | flops 20000000000 | bytes 60000000 | tf_op jit(solution)/shard_map/pallas_call | solution.py:472
  142.0 3.4 %shard_map.74 = bf16[256,6144]{1,0:T(8,128)(2,1)} custom-call(bf16[256,128]{1,0:T(8,128)(2,1)} %get-tuple-element.8.picker_ref, f32[256,128]{1,0:T(8,128)} %get-tuple-element.9.weight_ref, bf16[128,6144]{1,0:T(8,128)(2,1)} %get-tuple-element.10.rows_ref), custom_call_target="tpu_custom_call" | custom-call | tf_op jit(solution)/shard_map/pallas_call | solution.py:510

commit v5 on v4

--- a/solution.py
+++ b/solution.py
@@ -432,13 +432,9 @@
     sums(2, 0, 6)
     down(0, 1, 4, 2)
     sums(0, 0, 0)
-    down(0, 0, 4, 2)
+    for rz, ryl in ((1, 1), (3, 1), (1, 0), (3, 0)):
+        down(rz, ryl, 6, 1)
     sums(0, 1, 4)
-    sums(0, 0, 4)
-    for rz, ryl in ((1, 1), (3, 1), (1, 0), (3, 0), (0, 1), (0, 0)):
-        down(rz, ryl, 6, 1)
-    sums(0, 1, 6)
-    sums(0, 0, 6)
     arrived(*d_pr)
     for rz in (2, 3, 1, 0):
         down(rz, 1, 7, 1)
@@ -448,13 +444,19 @@
         sums(rz, ryl, 6)
     for rz in (2, 3, 1, 0):
         down(rz, 0, 7, 1)
+    down(0, 0, 4, 2)
+    down(0, 1, 6, 1)
+    down(0, 0, 6, 1)
     sums(2, 0, 7)
     to_y(4, 2)
+    sums(0, 0, 4)
+    sums(0, 1, 6)
+    sums(0, 0, 6)
     sums(3, 0, 7)
     sums(1, 0, 7)
     sums(0, 0, 7)
+    to_y(6, 1)
     rows_out(0, 4)
-    to_y(6, 1)
     rows_out(4, 2)
     rows_out(7, 1)
     rows_out(6, 1)

time: 146 us -> 146 us (level)
  no operation moved by 1% of the time
where the time goes in v5:
time: 146 us; the launch traced here: 145 us
  Pallas kernels  145 us (99%)
    pallas_call x1, Pallas kernels, body(): pl.pallas_call(kernel, out_shape=(jax.ShapeDtypeStruct((2 * SLOTS, tokens...  142 us
    pallas_call x1, Pallas kernels, body(): pl.pallas_call(combine, grid=(2,), out_shape=jax.ShapeDtypeStruct(tokens....  3.44 us

profile of v5, /device:TPU:0, one launch (start us, length us, event | category | flops | bytes accessed | tf_op | source)
XLA Modules:
  0.0 145.5 jit_solution(11025941669463128974)
XLA Ops:
  0.0 142.0 %shard_map.73 = (bf16[128,6144]{1,0:T(8,128)(2,1)}, bf16[256,128]{1,0:T(8,128)(2,1)}, f32[256,128]{1,0:T(8,128)}) custom-call(bf16[256,6144]{1,0:T(8,128)(2,1)} %tok_hbm.1, s32[2,256]{1,0:T(2,128)} %bitcast.3, s32[2,256]{1,0:T(2,128)} %bitcast.4, f32[2,256]{1,0:T(2,128)} %bitcast.5, bf16[768,512]{1,0:T(8,128)(2,1)} %wg_hbm.1, bf16[768,512]{1,0:T(8,128)(2,1)} %wu_hbm.1, ...), custom_call_target="tpu_custom_call" | custom-call | flops 20000000000 | bytes 60000000 | tf_op jit(solution)/shard_map/pallas_call | solution.py:474
  142.0 3.4 %shard_map.74 = bf16[256,6144]{1,0:T(8,128)(2,1)} custom-call(bf16[256,128]{1,0:T(8,128)(2,1)} %get-tuple-element.8.picker_ref, f32[256,128]{1,0:T(8,128)} %get-tuple-element.9.weight_ref, bf16[128,6144]{1,0:T(8,128)(2,1)} %get-tuple-element.10.rows_ref), custom_call_target="tpu_custom_call" | custom-call | tf_op jit(solution)/shard_map/pallas_call | solution.py:512
